TPU v7x, 256 devices: a whole 4x4x8 slice. The times are simulated.
256 devices in a mesh: seq: 64 (over z, x, core), head: 4 (over y).
Axes of the slice: x: 4, y: 4, z: 8, core: 2. Of those that a mesh axis runs over, the one named last changes fastest.
Arguments:
- video_q: bfloat16 [8192, 2048], P('seq', 'head'), may hold values from -7.5 to 7.5
- video_k: bfloat16 [8192, 2048], P('seq', 'head'), may hold values from -7.5 to 7.5
- video_v: bfloat16 [8192, 2048], P('seq', 'head'), may hold values from -24 to 24
- audio_q: bfloat16 [512, 2048], P('seq', 'head'), may hold values from -7.5 to 7.5
- audio_k: bfloat16 [512, 2048], P('seq', 'head'), may hold values from -7.5 to 7.5
- audio_v: bfloat16 [512, 2048], P('seq', 'head'), may hold values from -24 to 24
- video_lengths: int32 [4], replicated, may hold values from 1 to 3584, 8192 in all
- audio_lengths: int32 [4], replicated, may hold values from 1 to 224, 512 in all
- video_out_weight: bfloat16 [2048, 4096], P(None, 'head'), may hold values from -0.125 to 0.125
- audio_out_weight: bfloat16 [2048, 2048], P(None, 'head'), may hold values from -0.125 to 0.125
Outputs:
- video_out: bfloat16 [8192, 4096], P('seq', 'head')
- audio_out: bfloat16 [512, 2048], P('seq', 'head')
Inputs may be any that keep to these rules, and one draw needn't show every extreme that they name: `video_lengths`: clips lie end to end in order; one clip has exactly 3584 video tokens. `audio_lengths`: clips lie end to end in order; one clip has exactly 224 audio tokens.
All inputs are finite; a program needn't handle non-finite values.
Results may differ from a plain program's by a relative error of at most 0.012.
Values may be sent and summed in bfloat16 or wider, within the bound.
A program may use at most 64 MiB of HBM per device.

v0:
```python
import math
import jax
import jax.numpy as jnp
from jax import lax
from jax.sharding import Mesh
from jax.sharding import PartitionSpec as P

HEAD_DIM = 64
SEQ = ("seq_0", "seq_1", "seq_2")
masked_floor = -1e30


def sent_to_all(value, axis):
    count = lax.axis_size(axis)
    return lax.all_to_all(
        jnp.broadcast_to(value[None], (count, *value.shape)), axis, 0, 0, tiled=True
    )


def in_order(pieces, dim):
    pieces = jnp.moveaxis(pieces, 0, dim)
    dims = pieces.shape
    return pieces.reshape(*dims[:dim], dims[dim] * dims[dim + 1], *dims[dim + 2 :])


def gather_axes(value, axes, dim):
    far, near = axes
    first = sent_to_all(value, far)
    pieces = jnp.swapaxes(sent_to_all(first, near), 0, 1)
    return in_order(pieces.reshape(-1, *value.shape), dim)


def sent_together(arrays, axis, dim, along):
    both = jnp.concatenate(arrays, axis=along)
    filled, at, finished = (gather_axes(both, axis, dim), 0, [])
    for a in arrays:
        finished.append(lax.slice_in_dim(filled, at, at + a.shape[along], axis=along))
        at += a.shape[along]
    return tuple(finished)


def taken_together(value, axis):
    return sent_to_all(value, axis).max(axis=0)


def in_blocks(value, dim, count):
    dims = value.shape
    pieces = value.reshape(*dims[:dim], count, dims[dim] // count, *dims[dim + 1 :])
    return jnp.moveaxis(pieces, dim, 0)


def sum_at_owner(value, axis, dim):
    count = lax.axis_size(axis)
    pieces = lax.all_to_all(in_blocks(value, dim, count), axis, 0, 0, tiled=True)
    return jnp.sum(pieces, axis=0)


def sum_by_axis(value, axes, dim):
    far, near = axes
    own = sum_at_owner(in_blocks(value, dim, lax.axis_size(far)), near, dim + 1)
    return jnp.sum(lax.all_to_all(own, far, 0, 0, tiled=True), axis=0)


def sent_together_2(arrays, axis, dim, along):
    both = jnp.concatenate(arrays, axis=along)
    filled, at, finished = (sum_by_axis(both, axis, dim), 0, [])
    for a in arrays:
        finished.append(lax.slice_in_dim(filled, at, at + a.shape[along], axis=along))
        at += a.shape[along]
    return tuple(finished)


def gathered_copies(value, axis, dim):
    pieces = sent_to_all(value, axis)
    return in_order(pieces, dim)


def clip_index(positions, lengths):
    clip_ends = jnp.cumsum(lengths)
    return jnp.sum((positions[:, None] >= clip_ends[None, :]).astype(jnp.int32), axis=1)


def audio_clips(stored, audio_total, lengths):
    positions = (stored + audio_total // 2) % audio_total
    return clip_index(positions, lengths)


def per_device(
    video_q,
    video_k,
    video_v,
    audio_q,
    audio_k,
    audio_v,
    video_lengths,
    audio_lengths,
    video_out_weight,
    audio_out_weight,
):
    seq_count = lax.axis_size(SEQ)
    seq_rank = lax.axis_index(SEQ)
    video_rows, local_width = video_q.shape
    audio_rows = audio_q.shape[0]
    local_heads = local_width // HEAD_DIM
    audio_total = audio_rows * seq_count
    score_scale = 1.0 / math.sqrt(HEAD_DIM)
    video_clip = clip_index(
        seq_rank * video_rows + jnp.arange(video_rows, dtype=jnp.int32), video_lengths
    )
    query_clip = audio_clips(jnp.arange(audio_total, dtype=jnp.int32), audio_total, audio_lengths)
    every_query, every_key, every_value = sent_together(
        (audio_q, audio_k, audio_v), (("seq_0", "seq_1"), "seq_2"), 0, 1
    )
    query_heads = video_q.reshape(video_rows, local_heads, HEAD_DIM)
    scores = (
        jnp.einsum(
            "qhd,khd->qhk",
            query_heads,
            every_key.reshape(audio_total, local_heads, HEAD_DIM),
            preferred_element_type=jnp.float32,
        )
        * score_scale
    )
    allowed = video_clip[:, None, None] == query_clip[None, None, :]
    scores = jnp.where(allowed, scores, masked_floor)
    row_max = jnp.max(scores, axis=2, keepdims=True)
    weights = jnp.where(allowed, jnp.exp(scores - row_max), 0.0)
    video_totals = jnp.sum(weights, axis=2)
    video_mixed = jnp.einsum(
        "qhk,khd->qhd",
        weights.astype(jnp.bfloat16),
        every_value.reshape(audio_total, local_heads, HEAD_DIM),
        preferred_element_type=jnp.float32,
    )
    video_attn = (
        (video_mixed / video_totals[:, :, None])
        .reshape(video_rows, local_width)
        .astype(jnp.bfloat16)
    )
    video_proj = jnp.dot(
        lax.all_gather(video_attn, "head", axis=1, tiled=True),
        video_out_weight,
        preferred_element_type=jnp.float32,
    )
    query_block = math.gcd(audio_total, 512)
    block_count = audio_total // query_block
    video_key_heads = video_k.reshape(video_rows, local_heads, HEAD_DIM)
    video_value_heads = video_v.reshape(video_rows, local_heads, HEAD_DIM)

    def partial_block(paired):
        query_part, clip_part = paired
        block_scores = (
            jnp.einsum(
                "qhd,khd->qhk",
                query_part.reshape(query_block, local_heads, HEAD_DIM),
                video_key_heads,
                preferred_element_type=jnp.float32,
            )
            * score_scale
        )
        permitted = clip_part[:, None, None] == video_clip[None, None, :]
        block_scores = jnp.where(permitted, block_scores, masked_floor)
        local_max = jnp.max(block_scores, axis=2)
        block_weights = jnp.where(permitted, jnp.exp(block_scores - local_max[:, :, None]), 0.0)
        totals = jnp.sum(block_weights, axis=2)
        weighted = jnp.einsum(
            "qhk,khd->qhd",
            block_weights.astype(jnp.bfloat16),
            video_value_heads,
            preferred_element_type=jnp.float32,
        ).reshape(query_block, local_width)
        return (local_max, totals, weighted)

    local_max, totals, weighted = lax.map(
        partial_block,
        (
            every_query.reshape(block_count, query_block, local_width),
            query_clip.reshape(block_count, query_block),
        ),
    )
    local_max = local_max.reshape(audio_total, local_heads)
    totals = totals.reshape(audio_total, local_heads)
    weighted = weighted.reshape(audio_total, local_width)
    global_max = taken_together(local_max, SEQ)
    factor = jnp.exp(local_max - global_max)
    scaled_sum = (
        weighted.reshape(audio_total, local_heads, HEAD_DIM) * factor[:, :, None]
    ).reshape(audio_total, local_width)
    own_sum, own_total = sent_together_2(
        (scaled_sum, totals * factor), (("seq_0", "seq_1"), "seq_2"), 0, 1
    )
    audio_attn = (
        (own_sum.reshape(audio_rows, local_heads, HEAD_DIM) / own_total[:, :, None])
        .reshape(audio_rows, local_width)
        .astype(jnp.bfloat16)
    )
    audio_full = gathered_copies(audio_attn, "head", 1)
    audio_proj = jnp.dot(audio_full, audio_out_weight, preferred_element_type=jnp.float32)
    return (video_proj.astype(jnp.bfloat16), audio_proj.astype(jnp.bfloat16))


def solution(mesh):
    finer = Mesh(
        mesh.devices.reshape(8, 4, 2, mesh.shape["head"]), ("seq_0", "seq_1", "seq_2", "head")
    )
    placed = (
        P(SEQ, "head"),
        P(SEQ, "head"),
        P(SEQ, "head"),
        P(SEQ, "head"),
        P(SEQ, "head"),
        P(SEQ, "head"),
        P(),
        P(),
        P(None, "head"),
        P(None, "head"),
    )
    return jax.shard_map(
        per_device,
        mesh=finer,
        in_specs=placed,
        out_specs=(P(SEQ, "head"), P(SEQ, "head")),
        check_vma=False,
    )
```

profile of v0, /device:TPU:2, one launch (start us, length us, event | category | flops | bytes accessed | tf_op | source)
XLA Modules:
  0.0 135.7 jit_solution(13302887809576837175)
XLA Ops:
  0.7 0.9 pad_maximum_fusion
  1.6 0.9 broadcast_in_dim.91
  2.5 11.6 %all-to-all-start = ((bf16[32,8,1536]{2,1,0:T(8,128)(2,1)}), bf16[32,8,1536]{2,1,0:T(8,128)(2,1)S(1)}, u32[]{:S(2)}, u32[]{:S(2)}) async-start(bf16[32,8,1536]{2,1,0:T(8,128)(2,1)} %broadcast_in_dim.91), calls=%async_computation | async-start | bytes 1572864 | tf_op jit(solution)/shard_map/all_to_all | solution.py:15
  15.0 21.6 %all-to-all-done = bf16[32,8,1536]{2,1,0:T(8,128)(2,1)S(1)} async-done(((bf16[32,8,1536]{2,1,0:T(8,128)(2,1)}), bf16[32,8,1536]{2,1,0:T(8,128)(2,1)S(1)}, u32[]{:S(2)}, u32[]{:S(2)}) %all-to-all-start) | async-done | bytes 786464 | tf_op jit(solution)/shard_map/all_to_all | solution.py:15
  36.7 5.0 %all_to_all.30 = bf16[2,32,8,1536]{3,2,1,0:T(8,128)(2,1)S(1)} all-to-all(bf16[2,32,8,1536]{3,2,1,0:T(8,128)(2,1)S(1)} %broadcast_in_dim.92), channel_id=1, replica_groups=mesh['seq_0'=8,'seq_1'=4,'seq_2'=2,'head'=4] {'seq_2'}, dimensions={0} | all-to-all | bytes 3145728 | tf_op jit(solution)/shard_map/all_to_all | solution.py:15
  41.7 0.2 copy.42
  41.9 1.1 fusion.36
  43.0 0.2 copy.47
  43.2 1.9 %bitcast_reduce_fusion = (f32[512,8]{0,1:T(8,128)S(1)}, f32[8,512,128]{2,1,0:T(8,128)}) fusion(pred[512,128]{1,0:T(8,128)(4,1)S(1)} %broadcast_compare_fusion, bf16[512,8,64]{0,2,1:T(8,128)(2,1)S(1)} %bitcast.66, bf16[128,8,64]{0,2,1:T(8,128)(2,1)S(1)} %bitcast.70), kind=kOutput, calls=%fused_computation.2 | convolution fusion | flops 68677632 | bytes 2834432 | tf_op jit(solution)/shard_map/while/body/eval_jaxpr/qhd,khd->qhk/dot_general | solution.py:153
  45.1 1.1 broadcast_in_dim.100
  46.2 6.0 %all-to-all-start.2 = ((f32[64,512,8]{1,2,0:T(8,128)}), f32[64,512,8]{1,2,0:T(8,128)S(1)}, u32[]{:S(2)}, u32[]{:S(2)}) async-start(f32[64,512,8]{1,2,0:T(8,128)} %broadcast_in_dim.100), calls=%async_computation.2 | async-start | bytes 2097152 | tf_op jit(solution)/shard_map/all_to_all | solution.py:15
  52.2 0.8 copy.50
  52.9 2.5 %fusion.4 = f32[512,8]{0,1:T(8,128)S(1)} fusion(f32[8,512,128]{2,1,0:T(8,128)} %get-tuple-element.26, f32[512,8]{0,1:T(8,128)S(1)} %get-tuple-element.25, pred[512,128]{1,0:T(8,128)(4,1)S(1)} %broadcast_compare_fusion), kind=kLoop, calls=%fused_computation.9 | loop fusion | flops 2617344 | bytes 2195456 | tf_op jit(solution)/shard_map/while/body/eval_jaxpr/reduce_sum | solution.py:165
  55.5 25.5 %all-to-all-done.2 = f32[64,512,8]{1,2,0:T(8,128)S(1)} async-done(((f32[64,512,8]{1,2,0:T(8,128)}), f32[64,512,8]{1,2,0:T(8,128)S(1)}, u32[]{:S(2)}, u32[]{:S(2)}) %all-to-all-start.2) | async-done | bytes 1048608 | tf_op jit(solution)/shard_map/all_to_all | solution.py:15
  81.2 2.3 %fusion.6 = f32[512,8,64]{0,2,1:T(8,128)S(1)} fusion(bf16[128,8,64]{0,2,1:T(8,128)(2,1)} %bitcast.76, f32[8,512,128]{2,1,0:T(8,128)} %get-tuple-element.26, f32[512,8]{0,1:T(8,128)S(1)} %get-tuple-element.25, pred[512,128]{1,0:T(8,128)(4,1)S(1)} %broadcast_compare_fusion, f32[512,8]{0,1:T(8,128)S(1)} %get-tuple-element.21), kind=kOutput, calls=%fused_computation.12 | convolution fusion | flops 69992448 | bytes 3375104 | tf_op jit(solution)/shard_map/while/body/eval_jaxpr/qhk,khd->qhd/dot_general | solution.py:166
  83.5 2.0 %copy.51 = f32[512,8,64]{2,1,0:T(8,128)} copy(f32[512,8,64]{0,2,1:T(8,128)S(1)} %fusion.6) | data formatting | bytes 2097152 | tf_op jit(solution)/shard_map/mul | solution.py:187
  85.5 1.9 %mul.52 = f32[32,2,8,512]{3,2,1,0:T(8,128)S(1)} reshape(f32[512,8,64]{2,1,0:T(8,128)} %copy.51) | data formatting | bytes 2097152 | tf_op jit(solution)/shard_map/mul | solution.py:187
  87.6 4.8 %all_to_all.31 = f32[2,32,8,520]{3,2,1,0:T(8,128)S(1)} all-to-all(f32[2,32,8,520]{3,2,1,0:T(8,128)S(1)} %copy.53), channel_id=1, replica_groups=mesh['seq_0'=8,'seq_1'=4,'seq_2'=2,'head'=4] {'seq_2'}, dimensions={0} | all-to-all | bytes 2129920 | tf_op jit(solution)/shard_map/all_to_all | solution.py:54
  92.4 1.0 reduce_sum.59
  93.4 5.4 %all-to-all-start.4 = ((f32[32,8,520]{2,1,0:T(8,128)}), f32[32,8,520]{2,1,0:T(8,128)S(1)}, u32[]{:S(2)}, u32[]{:S(2)}) async-start(f32[32,8,520]{2,1,0:T(8,128)} %reduce_sum.59), calls=%async_computation.4 | async-start | bytes 1310720 | tf_op jit(solution)/shard_map/all_to_all | solution.py:61
  98.8 0.8 broadcast_compare_fusion.1
  99.7 2.1 %copy.43 = bf16[512,512]{0,1:T(8,128)(2,1)} copy(bf16[512,512]{1,0:T(8,128)(2,1)} %get-tuple-element.24) | data formatting | bytes 1048576 | tf_op jit(solution)/shard_map/slice | solution.py:37
  101.8 1.0 copy.44
  102.8 2.1 %fusion.37 = f32[128,8]{0,1:T(8,128)S(1)} fusion(pred[128,512]{0,1:T(8,128)(4,1)S(1)} %copy-done.6, bf16[512,8,64]{0,2,1:T(8,128)(2,1)} %bitcast.67, bf16[128,8,64]{0,2,1:T(8,128)(2,1)S(1)} %bitcast.72), kind=kOutput, calls=%fused_computation.54 | convolution fusion | flops 69730816 | bytes 724992 | tf_op jit(solution)/shard_map/sub | solution.py:127
  104.9 1.8 %fusion.38 = f32[8,512,128]{2,1,0:T(8,128)} fusion(bf16[512,8,64]{0,2,1:T(8,128)(2,1)S(1)} %bitcast.68, bf16[128,8,64]{0,2,1:T(8,128)(2,1)S(1)} %bitcast.73), kind=kOutput, calls=%fused_computation.55 | convolution fusion | flops 67108864 | bytes 2752512 | tf_op jit(solution)/shard_map/qhd,khd->qhk/dot_general | solution.py:116
  106.8 3.9 %fusion.8 = bf16[128,8,64]{0,2,1:T(8,128)(2,1)S(1)} fusion(bf16[512,8,64]{0,2,1:T(8,128)(2,1)} %bitcast.71, f32[8,512,128]{2,1,0:T(8,128)} %fusion.38, pred[128,512]{0,1:T(8,128)(4,1)S(1)} %copy-done.6, f32[128,8]{0,1:T(8,128)S(1)} %fusion.37), kind=kOutput, calls=%fused_computation.17 | convolution fusion | flops 69862912 | bytes 2822144 | tf_op jit(solution)/shard_map/qhk,khd->qhd/dot_general | solution.py:129
  110.6 13.3 %all_gather.3 = bf16[128,2048]{0,1:T(8,128)(2,1)S(1)} all-gather(bf16[128,512]{0,1:T(8,128)(2,1)S(1)} %bitcast.75), channel_id=1, replica_groups=mesh['seq_0'=8,'seq_1'=4,'seq_2'=2,'head'=4] {'head'}, dimensions={1}, use_global_device_ids=true | all-gather | bytes 655360 | tf_op jit(solution)/shard_map/all_gather | solution.py:141
  124.2 0.6 broadcast_in_dim.101
  124.8 4.4 %all-to-all-start.5 = ((bf16[4,8,512]{2,1,0:T(8,128)(2,1)}), bf16[4,8,512]{2,1,0:T(8,128)(2,1)S(1)}, u32[]{:S(2)}, u32[]{:S(2)}) async-start(bf16[4,8,512]{2,1,0:T(8,128)(2,1)} %broadcast_in_dim.101), calls=%async_computation.5 | async-start | bytes 65536 | tf_op jit(solution)/shard_map/all_to_all | solution.py:15
  129.2 3.6 %convolution_convert_fusion = bf16[128,1024]{1,0:T(8,128)(2,1)} fusion(bf16[128,2048]{0,1:T(8,128)(2,1)S(1)} %all_gather.3, bf16[2048,1024]{1,0:T(8,128)(2,1)} %param.18), kind=kOutput, calls=%fused_computation.14 | convolution fusion | flops 537001984 | bytes 4980736 | tf_op jit(solution)/shard_map/dot_general | solution.py:140
  132.9 1.8 %all-to-all-done.5 = bf16[4,8,512]{2,1,0:T(8,128)(2,1)S(1)} async-done(((bf16[4,8,512]{2,1,0:T(8,128)(2,1)}), bf16[4,8,512]{2,1,0:T(8,128)(2,1)S(1)}, u32[]{:S(2)}, u32[]{:S(2)}) %all-to-all-start.5) | async-done | bytes 32800 | tf_op jit(solution)/shard_map/all_to_all | solution.py:15
  134.7 1.0 convolution_convert_fusion.1
  (39 shorter events, 1.7 us)
Async XLA Ops:
  0.6 134.0 %copy-start = (bf16[2048,512]{1,0:T(8,128)(2,1)S(1)}, bf16[2048,512]{1,0:T(8,128)(2,1)}, u32[]{:S(2)}) copy-start(bf16[2048,512]{1,0:T(8,128)(2,1)} %param.19) | copy-start | bytes 6291460
  0.6 13.5 %copy-start.7 = (s32[4]{0:T(128)S(1)}, s32[4]{0:T(128)}, u32[]{:S(2)}) copy-start(s32[4]{0:T(128)} %param.16) | copy-start | bytes 52
  0.7 13.7 %copy-start.8 = (s32[4]{0:T(128)S(1)}, s32[4]{0:T(128)}, u32[]{:S(2)}) copy-start(s32[4]{0:T(128)} %param.17) | copy-start | bytes 52
  0.7 13.8 %copy-start.3 = (bf16[128,512]{1,0:T(8,128)(2,1)S(1)}, bf16[128,512]{1,0:T(8,128)(2,1)}, u32[]{:S(2)}) copy-start(bf16[128,512]{1,0:T(8,128)(2,1)} %param.11) | copy-start | bytes 393220
  2.5 34.1 %all-to-all-start = ((bf16[32,8,1536]{2,1,0:T(8,128)(2,1)}), bf16[32,8,1536]{2,1,0:T(8,128)(2,1)S(1)}, u32[]{:S(2)}, u32[]{:S(2)}) async-start(bf16[32,8,1536]{2,1,0:T(8,128)(2,1)} %broadcast_in_dim.91), calls=%async_computation | async-start | bytes 1572864 | tf_op jit(solution)/shard_map/all_to_all | solution.py:15
  45.1 7.1 %copy-start.4 = (bf16[128,512]{1,0:T(8,128)(2,1)S(1)}, bf16[128,512]{1,0:T(8,128)(2,1)}, u32[]{:S(2)}) copy-start(bf16[128,512]{1,0:T(8,128)(2,1)} %param.12) | copy-start | bytes 393220
  46.2 34.8 %all-to-all-start.2 = ((f32[64,512,8]{1,2,0:T(8,128)}), f32[64,512,8]{1,2,0:T(8,128)S(1)}, u32[]{:S(2)}, u32[]{:S(2)}) async-start(f32[64,512,8]{1,2,0:T(8,128)} %broadcast_in_dim.100), calls=%async_computation.2 | async-start | bytes 2097152 | tf_op jit(solution)/shard_map/all_to_all | solution.py:15
  92.4 7.2 %copy-start.5 = (bf16[128,512]{1,0:T(8,128)(2,1)S(1)}, bf16[128,512]{1,0:T(8,128)(2,1)}, u32[]{:S(2)}) copy-start(bf16[128,512]{1,0:T(8,128)(2,1)} %param.10) | copy-start | bytes 393220
  93.4 8.4 %copy-start.1 = (bf16[512,512]{1,0:T(8,128)(2,1)S(1)}, bf16[512,512]{1,0:T(8,128)(2,1)}, u32[]{:S(2)}) copy-start(bf16[512,512]{1,0:T(8,128)(2,1)} %get-tuple-element.23) | copy-start | bytes 1572868
  93.4 30.5 %all-to-all-start.4 = ((f32[32,8,520]{2,1,0:T(8,128)}), f32[32,8,520]{2,1,0:T(8,128)S(1)}, u32[]{:S(2)}, u32[]{:S(2)}) async-start(f32[32,8,520]{2,1,0:T(8,128)} %reduce_sum.59), calls=%async_computation.4 | async-start | bytes 1310720 | tf_op jit(solution)/shard_map/all_to_all | solution.py:61
  99.7 3.1 %copy-start.6 = (pred[128,512]{0,1:T(8,128)(4,1)S(1)}, pred[128,512]{0,1:T(8,128)(4,1)}, u32[]{:S(2)}) copy-start(pred[128,512]{0,1:T(8,128)(4,1)} %broadcast_compare_fusion.1) | copy-start | bytes 196612
  102.8 2.1 %copy-start.2 = (bf16[512,512]{0,1:T(8,128)(2,1)S(1)}, bf16[512,512]{0,1:T(8,128)(2,1)}, u32[]{:S(2)}) copy-start(bf16[512,512]{0,1:T(8,128)(2,1)} %copy.44) | copy-start | bytes 1572868
  124.8 9.9 %all-to-all-start.5 = ((bf16[4,8,512]{2,1,0:T(8,128)(2,1)}), bf16[4,8,512]{2,1,0:T(8,128)(2,1)S(1)}, u32[]{:S(2)}, u32[]{:S(2)}) async-start(bf16[4,8,512]{2,1,0:T(8,128)(2,1)} %broadcast_in_dim.101), calls=%async_computation.5 | async-start | bytes 65536 | tf_op jit(solution)/shard_map/all_to_all | solution.py:15
where the time goes:
time: 136 us
  waiting for transfers between devices  48.9 us (36%)
  starting transfers between devices  27.4 us (20%)
  blocking collectives  23.1 us (17%)
  matrix products  16.6 us (12%)
  local copies, waits for them, and re-layouts  12.7 us (9%)
  other arithmetic  6.14 us (5%)
    all_to_all x3, waiting for transfers between devices, sent_to_all(): lax.all_to_all(jnp.broadcast_to(value[None], (count, *value.shape)), axis...  48.9 us
    all_to_all x3, starting transfers between devices, sent_to_all(): lax.all_to_all(jnp.broadcast_to(value[None], (count, *value.shape)), axis...  22 us
    all_gather x1, blocking collectives, per_device(): lax.all_gather(video_attn, 'head', axis=1, tiled=True)  13.3 us
    all_to_all x1, starting transfers between devices, sum_by_axis(): return jnp.sum(lax.all_to_all(own, far, 0, 0, tiled=True), axis=0)  5.38 us
    all_to_all x1, blocking collectives, sent_to_all(): lax.all_to_all(jnp.broadcast_to(value[None], (count, *value.shape)), axis...  5 us
    all_to_all x1, blocking collectives, sum_at_owner(): lax.all_to_all(in_blocks(value, dim, count), axis, 0, 0, tiled=True)  4.79 us
    slice x4, local copies, waits for them, and re-layouts, sent_together(): lax.slice_in_dim(filled, at, at + a.shape[along], axis=along)  4.41 us
    mul x2, local copies, waits for them, and re-layouts, per_device(): weighted.reshape(audio_total, local_heads, HEAD_DIM) * factor[:, :, None]  3.92 us
  transfers between devices with their start and end apart: 4, of which 3 were waited for; matrix products, arithmetic and copies ran while one was open for 14% of the time, Pallas kernels for 0%

commit v1 on v0

--- a/solution.py
+++ b/solution.py
@@ -138,7 +138,9 @@
         .astype(jnp.bfloat16)
     )
     video_proj = jnp.dot(
-        lax.all_gather(video_attn, "head", axis=1, tiled=True),
+        jnp.concatenate(
+            lax.all_to_all(jnp.stack([video_attn] * lax.axis_size("head")), "head", 0, 0), axis=1
+        ),
         video_out_weight,
         preferred_element_type=jnp.float32,
     )

time: 136 us -> 143 us (1.051)
  waiting for transfers between devices: 48.9 us -> 65.5 us
  blocking collectives: 23.1 us -> 9.78 us
  starting transfers between devices: 27.4 us -> 30.7 us
    all_gather x1 -> x0, blocking collectives: 13.3 us -> none  [per_device(): lax.all_gather(video_attn, 'head', axis=1, tiled=True)]
    all_to_all x1, waiting for transfers between devices: 0.01 us -> 8.77 us  [sum_by_axis(): return jnp.sum(lax.all_to_all(own, far, 0, 0, tiled=True), axis=0)]
    all_to_all x0 -> x1, waiting for transfers between devices: none -> 7.86 us  [per_device(): lax.all_to_all(jnp.stack([video_attn] * lax.axis_size('head')), 'head', 0...]
    all_to_all x0 -> x1, starting transfers between devices: none -> 4.46 us  [per_device(): lax.all_to_all(jnp.stack([video_attn] * lax.axis_size('head')), 'head', 0...]
  transfers between devices with their start and end apart: 4 -> 5, of which waited for: 3 -> 5; matrix products, arithmetic and copies ran while one was open for 14% -> 13% of each run, Pallas kernels for 0% -> 0%
where the time goes in v1:
time: 143 us; the launch traced here: 142 us
  waiting for transfers between devices  65.5 us (46%)
  starting transfers between devices  30.7 us (21%)
  matrix products  16.6 us (12%)
  local copies, waits for them, and re-layouts  13.5 us (9%)
  blocking collectives  9.78 us (7%)
  other arithmetic  5.52 us (4%)
    all_to_all x3, waiting for transfers between devices, sent_to_all(): lax.all_to_all(jnp.broadcast_to(value[None], (count, *value.shape)), axis...  48.9 us
    all_to_all x3, starting transfers between devices, sent_to_all(): lax.all_to_all(jnp.broadcast_to(value[None], (count, *value.shape)), axis...  20.8 us
    all_to_all x1, waiting for transfers between devices, sum_by_axis(): return jnp.sum(lax.all_to_all(own, far, 0, 0, tiled=True), axis=0)  8.77 us
    all_to_all x1, waiting for transfers between devices, per_device(): lax.all_to_all(jnp.stack([video_attn] * lax.axis_size('head')), 'head', 0...  7.86 us
    all_to_all x1, starting transfers between devices, sum_by_axis(): return jnp.sum(lax.all_to_all(own, far, 0, 0, tiled=True), axis=0)  5.38 us
    all_to_all x1, blocking collectives, sent_to_all(): lax.all_to_all(jnp.broadcast_to(value[None], (count, *value.shape)), axis...  5 us
    all_to_all x1, blocking collectives, sum_at_owner(): lax.all_to_all(in_blocks(value, dim, count), axis, 0, 0, tiled=True)  4.79 us
    all_to_all x1, starting transfers between devices, per_device(): lax.all_to_all(jnp.stack([video_attn] * lax.axis_size('head')), 'head', 0...  4.46 us
  transfers between devices with their start and end apart: 5, of which 5 were waited for; matrix products, arithmetic and copies ran while one was open for 13% of the time, Pallas kernels for 0%

profile of v1, /device:TPU:2, one launch (start us, length us, event | category | flops | bytes accessed | tf_op | source)
XLA Modules:
  0.0 142.4 jit_solution(1720540078618138357)
XLA Ops:
  0.7 0.9 pad_maximum_fusion
  1.6 0.9 broadcast_in_dim.91
  2.5 11.6 %all-to-all-start = ((bf16[32,8,1536]{2,1,0:T(8,128)(2,1)}), bf16[32,8,1536]{2,1,0:T(8,128)(2,1)S(1)}, u32[]{:S(2)}, u32[]{:S(2)}) async-start(bf16[32,8,1536]{2,1,0:T(8,128)(2,1)} %broadcast_in_dim.91), calls=%async_computation | async-start | bytes 1572864 | tf_op jit(solution)/shard_map/all_to_all | solution.py:15
  15.0 21.6 %all-to-all-done = bf16[32,8,1536]{2,1,0:T(8,128)(2,1)S(1)} async-done(((bf16[32,8,1536]{2,1,0:T(8,128)(2,1)}), bf16[32,8,1536]{2,1,0:T(8,128)(2,1)S(1)}, u32[]{:S(2)}, u32[]{:S(2)}) %all-to-all-start) | async-done | bytes 786464 | tf_op jit(solution)/shard_map/all_to_all | solution.py:15
  36.7 5.0 %all_to_all.35 = bf16[2,32,8,1536]{3,2,1,0:T(8,128)(2,1)S(1)} all-to-all(bf16[2,32,8,1536]{3,2,1,0:T(8,128)(2,1)S(1)} %broadcast_in_dim.92), channel_id=1, replica_groups=mesh['seq_0'=8,'seq_1'=4,'seq_2'=2,'head'=4] {'seq_2'}, dimensions={0} | all-to-all | bytes 3145728 | tf_op jit(solution)/shard_map/all_to_all | solution.py:15
  41.9 1.1 fusion.36
  43.2 1.9 %bitcast_reduce_fusion = (f32[512,8]{0,1:T(8,128)S(1)}, f32[8,512,128]{2,1,0:T(8,128)}) fusion(pred[512,128]{1,0:T(8,128)(4,1)S(1)} %broadcast_compare_fusion, bf16[512,8,64]{0,2,1:T(8,128)(2,1)S(1)} %bitcast.70, bf16[128,8,64]{0,2,1:T(8,128)(2,1)S(1)} %bitcast.74), kind=kOutput, calls=%fused_computation.2 | convolution fusion | flops 68677632 | bytes 2834432 | tf_op jit(solution)/shard_map/while/body/eval_jaxpr/qhd,khd->qhk/dot_general | solution.py:155
  45.1 1.1 broadcast_in_dim.100
  46.2 6.0 %all-to-all-start.3 = ((f32[64,512,8]{1,2,0:T(8,128)}), f32[64,512,8]{1,2,0:T(8,128)S(1)}, u32[]{:S(2)}, u32[]{:S(2)}) async-start(f32[64,512,8]{1,2,0:T(8,128)} %broadcast_in_dim.100), calls=%async_computation.3 | async-start | bytes 2097152 | tf_op jit(solution)/shard_map/all_to_all | solution.py:15
  52.2 0.8 copy.51
  52.9 2.5 %fusion.4 = f32[512,8]{0,1:T(8,128)S(1)} fusion(f32[8,512,128]{2,1,0:T(8,128)} %get-tuple-element.26, f32[512,8]{0,1:T(8,128)S(1)} %get-tuple-element.25, pred[512,128]{1,0:T(8,128)(4,1)S(1)} %broadcast_compare_fusion), kind=kLoop, calls=%fused_computation.9 | loop fusion | flops 2617344 | bytes 2195456 | tf_op jit(solution)/shard_map/while/body/eval_jaxpr/reduce_sum | solution.py:167
  55.5 25.5 %all-to-all-done.3 = f32[64,512,8]{1,2,0:T(8,128)S(1)} async-done(((f32[64,512,8]{1,2,0:T(8,128)}), f32[64,512,8]{1,2,0:T(8,128)S(1)}, u32[]{:S(2)}, u32[]{:S(2)}) %all-to-all-start.3) | async-done | bytes 1048608 | tf_op jit(solution)/shard_map/all_to_all | solution.py:15
  81.2 2.3 %fusion.6 = f32[512,8,64]{0,2,1:T(8,128)S(1)} fusion(bf16[128,8,64]{0,2,1:T(8,128)(2,1)} %bitcast.80, f32[8,512,128]{2,1,0:T(8,128)} %get-tuple-element.26, f32[512,8]{0,1:T(8,128)S(1)} %get-tuple-element.25, pred[512,128]{1,0:T(8,128)(4,1)S(1)} %broadcast_compare_fusion, f32[512,8]{0,1:T(8,128)S(1)} %get-tuple-element.21), kind=kOutput, calls=%fused_computation.12 | convolution fusion | flops 69992448 | bytes 3375104 | tf_op jit(solution)/shard_map/while/body/eval_jaxpr/qhk,khd->qhd/dot_general | solution.py:168
  83.5 2.0 %copy.52 = f32[512,8,64]{2,1,0:T(8,128)} copy(f32[512,8,64]{0,2,1:T(8,128)S(1)} %fusion.6) | data formatting | bytes 2097152 | tf_op jit(solution)/shard_map/mul | solution.py:189
  85.5 1.9 %mul.52 = f32[32,2,8,512]{3,2,1,0:T(8,128)S(1)} reshape(f32[512,8,64]{2,1,0:T(8,128)} %copy.52) | data formatting | bytes 2097152 | tf_op jit(solution)/shard_map/mul | solution.py:189
  87.6 4.8 %all_to_all.36 = f32[2,32,8,520]{3,2,1,0:T(8,128)S(1)} all-to-all(f32[2,32,8,520]{3,2,1,0:T(8,128)S(1)} %copy.54), channel_id=1, replica_groups=mesh['seq_0'=8,'seq_1'=4,'seq_2'=2,'head'=4] {'seq_2'}, dimensions={0} | all-to-all | bytes 2129920 | tf_op jit(solution)/shard_map/all_to_all | solution.py:54
  92.4 1.0 reduce_sum.59
  93.4 5.4 %all-to-all-start.5 = ((f32[32,8,520]{2,1,0:T(8,128)}), f32[32,8,520]{2,1,0:T(8,128)S(1)}, u32[]{:S(2)}, u32[]{:S(2)}) async-start(f32[32,8,520]{2,1,0:T(8,128)} %reduce_sum.59), calls=%async_computation.5 | async-start | bytes 1310720 | tf_op jit(solution)/shard_map/all_to_all | solution.py:61
  99.1 2.1 %copy.44 = bf16[512,512]{0,1:T(8,128)(2,1)} copy(bf16[512,512]{1,0:T(8,128)(2,1)} %get-tuple-element.24) | data formatting | bytes 1048576 | tf_op jit(solution)/shard_map/slice | solution.py:37
  101.1 1.0 copy.45
  102.1 2.1 %fusion.37 = f32[128,8]{0,1:T(8,128)S(1)} fusion(pred[128,512]{0,1:T(8,128)(4,1)S(1)} %broadcast_compare_fusion.1, bf16[512,8,64]{0,2,1:T(8,128)(2,1)} %bitcast.71, bf16[128,8,64]{0,2,1:T(8,128)(2,1)S(1)} %bitcast.76), kind=kOutput, calls=%fused_computation.54 | convolution fusion | flops 69730816 | bytes 724992 | tf_op jit(solution)/shard_map/sub | solution.py:127
  104.3 1.8 %fusion.38 = f32[8,512,128]{2,1,0:T(8,128)} fusion(bf16[512,8,64]{0,2,1:T(8,128)(2,1)S(1)} %bitcast.72, bf16[128,8,64]{0,2,1:T(8,128)(2,1)S(1)} %bitcast.77), kind=kOutput, calls=%fused_computation.55 | convolution fusion | flops 67108864 | bytes 2752512 | tf_op jit(solution)/shard_map/qhd,khd->qhk/dot_general | solution.py:116
  106.1 3.9 %fusion.8 = bf16[128,8,64]{0,2,1:T(8,128)(2,1)S(1)} fusion(bf16[512,8,64]{0,2,1:T(8,128)(2,1)} %bitcast.75, f32[8,512,128]{2,1,0:T(8,128)} %fusion.38, pred[128,512]{0,1:T(8,128)(4,1)S(1)} %broadcast_compare_fusion.1, f32[128,8]{0,1:T(8,128)S(1)} %fusion.37), kind=kOutput, calls=%fused_computation.17 | convolution fusion | flops 69862912 | bytes 2822144 | tf_op jit(solution)/shard_map/qhk,khd->qhd/dot_general | solution.py:129
  110.0 8.8 %all-to-all-done.5 = f32[32,8,520]{2,1,0:T(8,128)S(1)} async-done(((f32[32,8,520]{2,1,0:T(8,128)}), f32[32,8,520]{2,1,0:T(8,128)S(1)}, u32[]{:S(2)}, u32[]{:S(2)}) %all-to-all-start.5) | async-done | bytes 532512 | tf_op jit(solution)/shard_map/all_to_all | solution.py:61
  118.7 0.9 stack.2
  119.6 4.5 %all-to-all-start.2 = ((bf16[4,128,512]{1,2,0:T(8,128)(2,1)}), bf16[4,128,512]{1,2,0:T(8,128)(2,1)S(1)}, u32[]{:S(2)}, u32[]{:S(2)}) async-start(bf16[4,128,512]{1,2,0:T(8,128)(2,1)} %stack.2), calls=%async_computation.2 | async-start | bytes 1048576 | tf_op jit(solution)/shard_map/all_to_all | solution.py:142
  124.3 7.9 %all-to-all-done.2 = bf16[4,128,512]{1,2,0:T(8,128)(2,1)S(1)} async-done(((bf16[4,128,512]{1,2,0:T(8,128)(2,1)}), bf16[4,128,512]{1,2,0:T(8,128)(2,1)S(1)}, u32[]{:S(2)}, u32[]{:S(2)}) %all-to-all-start.2) | async-done | bytes 524320 | tf_op jit(solution)/shard_map/all_to_all | solution.py:142
  132.1 0.6 broadcast_in_dim.101
  132.8 3.3 %all-to-all-start.6 = ((bf16[4,8,512]{2,1,0:T(8,128)(2,1)}), bf16[4,8,512]{2,1,0:T(8,128)(2,1)S(1)}, u32[]{:S(2)}, u32[]{:S(2)}) async-start(bf16[4,8,512]{2,1,0:T(8,128)(2,1)} %broadcast_in_dim.101), calls=%async_computation.6 | async-start | bytes 65536 | tf_op jit(solution)/shard_map/all_to_all | solution.py:15
  136.0 3.6 %convolution_convert_fusion = bf16[128,1024]{1,0:T(8,128)(2,1)} fusion(bf16[128,2048]{0,1:T(8,128)(2,1)S(1)} %bitcast.69, bf16[2048,1024]{1,0:T(8,128)(2,1)} %param.18), kind=kOutput, calls=%fused_computation.14 | convolution fusion | flops 537001984 | bytes 4980736 | tf_op jit(solution)/shard_map/dot_general | solution.py:140
  139.7 1.8 %all-to-all-done.6 = bf16[4,8,512]{2,1,0:T(8,128)(2,1)S(1)} async-done(((bf16[4,8,512]{2,1,0:T(8,128)(2,1)}), bf16[4,8,512]{2,1,0:T(8,128)(2,1)S(1)}, u32[]{:S(2)}, u32[]{:S(2)}) %all-to-all-start.6) | async-done | bytes 32800 | tf_op jit(solution)/shard_map/all_to_all | solution.py:15
  141.4 1.0 convolution_convert_fusion.1
  (39 shorter events, 2.2 us)
Async XLA Ops:
  0.6 140.8 %copy-start = (bf16[2048,512]{1,0:T(8,128)(2,1)S(1)}, bf16[2048,512]{1,0:T(8,128)(2,1)}, u32[]{:S(2)}) copy-start(bf16[2048,512]{1,0:T(8,128)(2,1)} %param.19) | copy-start | bytes 6291460
  0.6 13.5 %copy-start.6 = (s32[4]{0:T(128)S(1)}, s32[4]{0:T(128)}, u32[]{:S(2)}) copy-start(s32[4]{0:T(128)} %param.16) | copy-start | bytes 52
  0.7 13.7 %copy-start.7 = (s32[4]{0:T(128)S(1)}, s32[4]{0:T(128)}, u32[]{:S(2)}) copy-start(s32[4]{0:T(128)} %param.17) | copy-start | bytes 52
  0.7 13.8 %copy-start.3 = (bf16[128,512]{1,0:T(8,128)(2,1)S(1)}, bf16[128,512]{1,0:T(8,128)(2,1)}, u32[]{:S(2)}) copy-start(bf16[128,512]{1,0:T(8,128)(2,1)} %param.11) | copy-start | bytes 393220
  2.5 34.1 %all-to-all-start = ((bf16[32,8,1536]{2,1,0:T(8,128)(2,1)}), bf16[32,8,1536]{2,1,0:T(8,128)(2,1)S(1)}, u32[]{:S(2)}, u32[]{:S(2)}) async-start(bf16[32,8,1536]{2,1,0:T(8,128)(2,1)} %broadcast_in_dim.91), calls=%async_computation | async-start | bytes 1572864 | tf_op jit(solution)/shard_map/all_to_all | solution.py:15
  45.1 7.1 %copy-start.4 = (bf16[128,512]{1,0:T(8,128)(2,1)S(1)}, bf16[128,512]{1,0:T(8,128)(2,1)}, u32[]{:S(2)}) copy-start(bf16[128,512]{1,0:T(8,128)(2,1)} %param.12) | copy-start | bytes 393220
  46.2 34.8 %all-to-all-start.3 = ((f32[64,512,8]{1,2,0:T(8,128)}), f32[64,512,8]{1,2,0:T(8,128)S(1)}, u32[]{:S(2)}, u32[]{:S(2)}) async-start(f32[64,512,8]{1,2,0:T(8,128)} %broadcast_in_dim.100), calls=%async_computation.3 | async-start | bytes 2097152 | tf_op jit(solution)/shard_map/all_to_all | solution.py:15
  92.4 6.4 %copy-start.5 = (bf16[128,512]{1,0:T(8,128)(2,1)S(1)}, bf16[128,512]{1,0:T(8,128)(2,1)}, u32[]{:S(2)}) copy-start(bf16[128,512]{1,0:T(8,128)(2,1)} %param.10) | copy-start | bytes 393220
  93.4 7.7 %copy-start.1 = (bf16[512,512]{1,0:T(8,128)(2,1)S(1)}, bf16[512,512]{1,0:T(8,128)(2,1)}, u32[]{:S(2)}) copy-start(bf16[512,512]{1,0:T(8,128)(2,1)} %get-tuple-element.23) | copy-start | bytes 1572868
  93.4 25.3 %all-to-all-start.5 = ((f32[32,8,520]{2,1,0:T(8,128)}), f32[32,8,520]{2,1,0:T(8,128)S(1)}, u32[]{:S(2)}, u32[]{:S(2)}) async-start(f32[32,8,520]{2,1,0:T(8,128)} %reduce_sum.59), calls=%async_computation.5 | async-start | bytes 1310720 | tf_op jit(solution)/shard_map/all_to_all | solution.py:61
  102.1 2.1 %copy-start.2 = (bf16[512,512]{0,1:T(8,128)(2,1)S(1)}, bf16[512,512]{0,1:T(8,128)(2,1)}, u32[]{:S(2)}) copy-start(bf16[512,512]{0,1:T(8,128)(2,1)} %copy.45) | copy-start | bytes 1572868
  119.6 12.5 %all-to-all-start.2 = ((bf16[4,128,512]{1,2,0:T(8,128)(2,1)}), bf16[4,128,512]{1,2,0:T(8,128)(2,1)S(1)}, u32[]{:S(2)}, u32[]{:S(2)}) async-start(bf16[4,128,512]{1,2,0:T(8,128)(2,1)} %stack.2), calls=%async_computation.2 | async-start | bytes 1048576 | tf_op jit(solution)/shard_map/all_to_all | solution.py:142
  132.8 8.7 %all-to-all-start.6 = ((bf16[4,8,512]{2,1,0:T(8,128)(2,1)}), bf16[4,8,512]{2,1,0:T(8,128)(2,1)S(1)}, u32[]{:S(2)}, u32[]{:S(2)}) async-start(bf16[4,8,512]{2,1,0:T(8,128)(2,1)} %broadcast_in_dim.101), calls=%async_computation.6 | async-start | bytes 65536 | tf_op jit(solution)/shard_map/all_to_all | solution.py:15
